TPU v7x, 512 devices: a whole 4x4x16 slice. The times are simulated.
512 devices in a mesh: lag: 8 (over x, core), par: 64 (over z, y).
Axes of the slice: x: 4, y: 4, z: 16, core: 2. Of those that a mesh axis runs over, the one named last changes fastest.
Arguments:
- probes: bfloat16 [32, 64, 8192], P('lag', None, 'par'), may hold values from -6 to 6
- lag_blocks: bfloat16 [32, 512, 8192], P('lag', None, 'par'), may hold values from -0.0234375 to 0.0234375
- sensor_weights: float32 [512], replicated, may hold values from 0.2 to 2
- sensor_mask: int32 [512], replicated, may hold values 0 or 1
Outputs:
- hessian_probes: float32 [32, 64, 8192], P('lag', None, 'par')
- sensor_grad: float32 [512], replicated
All inputs are finite; a program needn't handle non-finite values.
Results may differ from a plain program's by a relative error of at most 0.0013.
Values may be sent and summed in bfloat16 or wider, within the bound.
A program may use at most 64 MiB of HBM per device.

v0:
```python
import jax
import jax.numpy as jnp
from jax import lax
from jax.sharding import PartitionSpec as P

NS = 512
PROBES = 64
LAG_DEV = 4


def per_device(probes, lag_blocks, sensor_weights, sensor_mask):
    width = probes.shape[2]
    time_steps = LAG_DEV * lax.axis_size("lag")
    lag_base = lax.axis_index("lag") * LAG_DEV
    stacked_blocks = lag_blocks.reshape(LAG_DEV * NS, width)
    active = sensor_mask.astype(jnp.float32)
    initial = jnp.zeros((2 * time_steps, PROBES, NS), jnp.float32)
    running = initial
    arrived = lax.all_gather(probes, "lag", axis=0, tiled=True)
    num_rows = arrived.shape[0]
    product = lax.dot_general(
        arrived.reshape(num_rows * PROBES, width),
        stacked_blocks,
        (((1,), (1,)), ((), ())),
        preferred_element_type=jnp.float32,
    )
    product = product.reshape(num_rows, PROBES, LAG_DEV, NS)
    for offset in range(LAG_DEV):
        position = lag_base + offset
        current = lax.dynamic_slice_in_dim(running, position, num_rows, 0)
        running = lax.dynamic_update_slice_in_dim(
            running, current + product[:, :, offset, :], position, 0
        )
    partial_obs = running[:time_steps]
    observed = lax.psum(partial_obs, ("lag", "par"))
    weighted = (sensor_weights * active * observed).astype(jnp.bfloat16)
    sensor_grad = active * jnp.sum(observed * observed, axis=(0, 1)) / (time_steps * PROBES)
    padded_weighted = jnp.concatenate([weighted, jnp.zeros_like(weighted)], 0)
    pieces = [
        lax.dynamic_slice_in_dim(
            padded_weighted, lag_base + offset, lax.axis_size("lag") * LAG_DEV, 0
        )
        for offset in range(LAG_DEV)
    ]
    joined = jnp.concatenate(pieces, axis=2).reshape(
        lax.axis_size("lag") * LAG_DEV * PROBES, LAG_DEV * NS
    )
    product = jnp.dot(joined, stacked_blocks, preferred_element_type=jnp.float32)
    misfit = lax.psum_scatter(
        product.reshape(lax.axis_size("lag") * LAG_DEV, PROBES, width),
        "lag",
        scatter_dimension=0,
        tiled=True,
    )
    hessian_probes = misfit + probes.astype(jnp.float32)
    return (hessian_probes, sensor_grad)


def solution(mesh):
    return jax.shard_map(
        per_device,
        mesh=mesh,
        in_specs=(P("lag", None, "par"), P("lag", None, "par"), P(), P()),
        out_specs=(P("lag", None, "par"), P()),
        check_vma=False,
    )
```

profile of v0, /device:TPU:1, one launch (start us, length us, event | category | flops | bytes accessed | tf_op | source)
XLA Modules:
  0.0 612.6 jit_solution(7369663759585095504)
XLA Ops:
  7.2 0.0 copy-start
  7.2 0.0 all-reduce.3.cloned.1.call-start
  7.2 20.2 %all_gather.3 = bf16[32,64,128]{2,1,0:T(8,128)(2,1)S(1)} all-gather(bf16[4,64,128]{2,1,0:T(8,128)(2,1)} %param.4), channel_id=1, replica_groups=mesh['lag'=8,'par'=64] {'lag'}, dimensions={0}, use_global_device_ids=true | all-gather | bytes 589824 | tf_op jit(solution)/shard_map/all_gather | solution.py:19
  27.4 0.0 copy-done
  27.4 8.1 %fusion.15 = f32[32,64,4,512]{3,1,2,0:T(8,128)} fusion(bf16[32,64,128]{2,1,0:T(8,128)(2,1)S(1)} %all_gather.3, bf16[4,512,128]{2,1,0:T(8,128)(2,1)S(1)} %copy-done), kind=kOutput, calls=%fused_computation.25 | convolution fusion | flops 1073741824 | bytes 17825792 | tf_op jit(solution)/shard_map/dot_general | solution.py:21
  35.5 4.3 broadcast_in_dim.2
  39.8 4.9 fusion.14
  44.6 6.8 %fusion.13 = f32[64,64,512]{2,1,0:T(8,128)} fusion(f32[64,64,512]{2,1,0:T(8,128)} %fusion.14, s32[]{:T(128)S(6)} %select_n.9, f32[32,64,4,512]{3,1,2,0:T(8,128)} %fusion.15), kind=kLoop, calls=%fused_computation.20 | loop fusion | flops 1048576 | bytes 12582916 | tf_op jit(solution)/shard_map/dynamic_update_slice | solution.py:31
  51.4 6.8 %fusion.11 = f32[64,64,512]{2,1,0:T(8,128)} fusion(f32[64,64,512]{2,1,0:T(8,128)} %fusion.13, s32[]{:T(128)S(6)} %select_n.10, f32[32,64,4,512]{3,1,2,0:T(8,128)} %fusion.15), kind=kLoop, calls=%fused_computation.17 | loop fusion | flops 1048576 | bytes 12582916 | tf_op jit(solution)/shard_map/dynamic_update_slice | solution.py:31
  58.2 6.8 %fusion.9 = f32[64,64,512]{2,1,0:T(8,128)} fusion(f32[64,64,512]{2,1,0:T(8,128)} %fusion.11, s32[]{:T(128)S(6)} %select_n.22, f32[32,64,4,512]{3,1,2,0:T(8,128)} %fusion.15), kind=kLoop, calls=%fused_computation.14 | loop fusion | flops 1048576 | bytes 12582916 | tf_op jit(solution)/shard_map/dynamic_update_slice | solution.py:31
  65.0 4.8 slice.24
  69.9 0.0 copy-start.2
  69.9 0.0 copy-start.3
  69.9 0.0 all-reduce.3.cloned.1.call-update
  69.9 0.0 reduce-scatter.2.cloned.1.call-start
  69.9 0.6 copy-done.2
  70.5 0.0 copy-done.3
  70.6 485.6 %all-reduce.3.cloned.1.call-done = f32[32,64,512]{2,1,0:T(8,128)} async-done(((f32[32,64,512]{2,1,0:T(8,128)}), f32[32,64,512]{2,1,0:T(8,128)}) %all-reduce.3.cloned.1.call-update) | async-done | bytes 4194320 | tf_op jit(solution)/shard_map/psum | solution.py:35
  556.2 3.0 multiply_reduce_fusion
  559.2 3.3 pad_dynamic-slice_fusion.3
  562.5 0.0 copy-start.1
  562.5 3.6 fusion
  566.1 0.0 reduce-scatter.2.cloned.1.call-update
  566.2 0.6 multiply_multiply_fusion
  566.7 37.4 %reduce-scatter.2.cloned.1.call-done = f32[4,64,128]{2,1,0:T(8,128)} async-done(((f32[32,64,128]{2,1,0:T(8,128)}), f32[4,64,128]{2,1,0:T(8,128)}) %reduce-scatter.2.cloned.1.call-update) | async-done | bytes 131088 | tf_op jit(solution)/shard_map/reduce_scatter | solution.py:49
  604.2 0.0 copy-done.1
  604.2 1.6 convert_add_fusion
  (1 shorter events, 0.0 us)
Async XLA Ops:
  7.2 20.2 %copy-start = (bf16[4,512,128]{2,1,0:T(8,128)(2,1)S(1)}, bf16[4,512,128]{2,1,0:T(8,128)(2,1)}, u32[]{:S(2)}) copy-start(bf16[4,512,128]{2,1,0:T(8,128)(2,1)} %param.5) | copy-start | bytes 1572868
  7.2 549.0 %all-reduce.3.cloned.1.call-start = ((), (), s32[]{:S(2)}) async-start(), calls=%async_computation.1 | async-start | bytes 8388608 | tf_op jit(solution)/shard_map/psum | solution.py:35
  69.9 0.7 copy-start.2
  69.9 0.7 copy-start.3
  69.9 534.3 %reduce-scatter.2.cloned.1.call-start = ((), (), s32[]{:S(2)}) async-start(), calls=%async_computation.2 | async-start | bytes 1179648 | tf_op jit(solution)/shard_map/reduce_scatter | solution.py:49
  562.5 41.7 %copy-start.1 = (bf16[4,64,128]{2,1,0:T(8,128)(2,1)S(1)}, bf16[4,64,128]{2,1,0:T(8,128)(2,1)}, u32[]{:S(2)}) copy-start(bf16[4,64,128]{2,1,0:T(8,128)(2,1)} %param.4) | copy-start | bytes 196612
Sparse Core Ops, SparseCore 0:
  70.0 486.1 all-reduce.2
  566.3 37.8 reduce-scatter.1
where the time goes:
time: 614 us; the launch traced here: 613 us
  waiting for transfers between devices  523 us (85%)
  other arithmetic  25.5 us (4%)
  blocking collectives  20.2 us (3%)
  local copies, waits for them, and re-layouts  18 us (3%)
  between operations  14.1 us (2%)
  matrix products  11.7 us (2%)
    psum x1, waiting for transfers between devices, per_device(): observed = lax.psum(partial_obs, ('lag', 'par'))  486 us
    reduce_scatter x1, waiting for transfers between devices, per_device(): lax.psum_scatter(product.reshape(lax.axis_size('lag') * LAG_DEV, PROBES,...  37.4 us
    dynamic_update_slice x3, other arithmetic, per_device(): lax.dynamic_update_slice_in_dim(running, current + product[:, :, offset,...  20.4 us
    all_gather x1, blocking collectives, per_device(): arrived = lax.all_gather(probes, 'lag', axis=0, tiled=True)  20.2 us
  transfers between devices with their start and end apart: 2, of which 2 were waited for; matrix products, arithmetic and copies ran while one was open for 0% of the time, Pallas kernels for 0%

commit v1 on v0

v1 whole, which is shorter than its diff:
```python
import functools

import jax
import jax.numpy as jnp
from jax import lax
from jax.experimental import pallas as pl
from jax.experimental.pallas import tpu as pltpu
from jax.sharding import PartitionSpec as P

MESH = pl.DeviceIdType.MESH
NS = 512
PROBES = 64
J = 4
Y = 4
F32 = jnp.float32
BF16 = jnp.bfloat16


def toeplitz_block(lags, d, sens):
    rows = []
    for b in range(J):
        parts = []
        for c in range(J):
            l = J * d + b - c
            if l < 0:
                parts.append(jnp.zeros((sens, lags.shape[-1]), BF16))
            else:
                parts.append(lags[l // J, l % J])
        rows.append(jnp.concatenate(parts, axis=1))
    return jnp.concatenate(rows, axis=0)


def kernel(
    R, Z, stop,
    probes_ref, lag_ref, weight_ref, mask_ref,
    out_ref, grad_ref,
    pbuf, lbuf, obs, ry, sz, rz, wz, wy, mis, md, send_x, mx, gsend, gbuf,
    local_sem, xs_sem, xr_sem, ps_sem, pr_sem, ys_sem, yr_sem, zs_sem, zr_sem,
    azs_sem, azr_sem, ays_sem, ayr_sem, ds_sem, dr_sem, ms_sem, mr_sem, gs_sem, gr_sem,
):
    r = lax.axis_index("lag")
    c = lax.axis_index("par")
    z, y = c // Y, lax.rem(c, Y)
    x, core = r // 2, lax.rem(r, 2)
    X = R // 2
    sens = NS // R
    npar = pbuf.shape[-1]

    lag_peer = lambda k: (lax.rem(r + k, R), c)
    y_peer = lambda k: (r, z * Y + lax.rem(y + k, Y))
    z_peer = lambda k: (r, lax.rem(z + k, Z) * Y + y)

    barrier = pltpu.get_barrier_semaphore()
    for peer, n in ((lag_peer, R), (y_peer, Y), (z_peer, Z)):
        for k in range(1, n):
            pl.semaphore_signal(barrier, inc=1, device_id=peer(k), device_id_type=MESH)
    pl.semaphore_wait(barrier, R + Y + Z - 3)

    sends = []

    def send(src, dst, ssem, rsem, dev):
        cp = pltpu.make_async_remote_copy(
            src_ref=src, dst_ref=dst, send_sem=ssem, recv_sem=rsem, device_id=dev, device_id_type=MESH
        )
        cp.start()
        sends.append(cp)
        return cp

    own_l = pltpu.make_async_copy(
        lag_ref.at[:, pl.ds(pl.multiple_of(r * sens, sens), sens), :], lbuf.at[r], local_sem.at[0]
    )
    own_p = pltpu.make_async_copy(probes_ref, pbuf.at[r], local_sem.at[1])
    own_l.start()
    own_p.start()
    first = []
    for k in range(1, R):
        q = lax.rem(r + k, R)
        first.append(send(probes_ref, pbuf.at[r], ps_sem.at[k], pr_sem.at[k], (q, c)))
        first.append(
            send(
                lag_ref.at[:, pl.ds(pl.multiple_of(q * sens, sens), sens), :],
                lbuf.at[r], xs_sem.at[k], xr_sem.at[k], (q, c),
            )
        )
    own_l.wait()
    own_p.wait()
    for cp in first:
        cp.wait_recv()

    if stop >= 1:
        for d in range(R):
            n = R - d
            lhs = jnp.concatenate([pbuf[:n, b].reshape(n * PROBES, npar) for b in range(J)], axis=1)
            rhs = toeplitz_block(lbuf, d, sens)
            term = lax.dot_general(lhs, rhs, (((1,), (1,)), ((), ())), preferred_element_type=F32)
            if d == 0:
                obs[...] = term
            else:
                obs[d * PROBES :, :] += term

    rows_y = obs.shape[0] // Y
    if stop >= 2:
        cps = []
        for k in range(1, Y):
            t = lax.rem(y + k, Y)
            cps.append(
                send(
                    obs.at[pl.ds(pl.multiple_of(t * rows_y, rows_y), rows_y), :],
                    ry.at[k - 1], ys_sem.at[k], yr_sem.at[k], y_peer(k),
                )
            )
        total = obs[pl.ds(pl.multiple_of(y * rows_y, rows_y), rows_y), :]
        for k in range(1, Y):
            cps[k - 1].wait_recv()
            total = total + ry[k - 1]
        for i in range(Z):
            sz[i] = total[16 * (i // 2) : 16 * (i // 2) + 16, 128 * (i % 2) : 128 * (i % 2) + 128]
    if stop >= 3:
        cps = []
        for k in range(1, Z):
            cps.append(
                send(sz.at[lax.rem(z + k, Z)], rz.at[k - 1], zs_sem.at[k], zr_sem.at[k], z_peer(k))
            )
        total = sz[z]
        for k in range(1, Z):
            cps[k - 1].wait_recv()
            total = total + rz[k - 1]

    half = 128 // sens
    row = weight_ref[pl.ds(r // half, 1), :] * mask_ref[pl.ds(r // half, 1), :].astype(F32)
    raw = weight_ref[pl.ds(r // half, 1), :]
    on = mask_ref[pl.ds(r // half, 1), :].astype(F32)

    def mine(v):
        swapped = jnp.concatenate([v[:, sens:], v[:, :sens]], axis=1)
        v = jnp.where(lax.rem(r, half) == 0, v, swapped)
        return v

    def both(v):
        return jnp.concatenate([v[:, :sens], v[:, :sens]], axis=1)

    if stop >= 4:
        wz[z] = (both(mine(row)) * total).astype(BF16)
        cps = []
        for k in range(1, Z):
            cps.append(send(wz.at[z], wz.at[z], azs_sem.at[k], azr_sem.at[k], z_peer(k)))
        for cp in cps:
            cp.wait_recv()
    if stop >= 5:
        cps = []
        for k in range(1, Y):
            cps.append(send(wz, wy.at[y], ays_sem.at[k], ayr_sem.at[k], y_peer(k)))
        wy[y] = wz[...]
        for cp in cps:
            cp.wait_recv()

    if stop >= 6:
        tot = jnp.zeros((1, 128), F32)
        for i in range(Y):
            for j in range(Z):
                w = wy[i, j].astype(F32)
                tot = tot + jnp.sum(w * w, axis=0, keepdims=True)
        tot = tot[:, :sens] + tot[:, sens:]
        wr = mine(raw)[:, :sens]
        g = mine(on)[:, :sens] * tot / (wr * wr) * (1.0 / (R * J * PROBES))
        g = jnp.concatenate([g, g], axis=1)
        gsend[...] = jnp.broadcast_to(g, (8, 128))
        gcps = []
        for k in range(1, R):
            gcps.append(send(gsend, gbuf.at[r], gs_sem.at[k], gr_sem.at[k], lag_peer(k)))
        gbuf[r] = gsend[...]

        def wrow(a):
            i, h = a * PROBES // rows_y, (a * PROBES % rows_y) // 16
            return jnp.concatenate(
                [jnp.concatenate([wy[i, 2 * (h + q)], wy[i, 2 * (h + q) + 1]], axis=1) for q in range(PROBES // 16)],
                axis=0,
            )

        wfull = [wrow(a) for a in range(R)]
        for d in range(R):
            n = R - d
            lhs = jnp.concatenate(wfull[d:], axis=0)
            rhs = toeplitz_block(lbuf, d, sens)
            term = jnp.dot(lhs, rhs, preferred_element_type=F32)
            for a in range(n):
                piece = term[a * PROBES : (a + 1) * PROBES]
                if d == 0:
                    mis[a % 2, a // 2] = piece
                else:
                    mis[a % 2, a // 2] += piece

    if stop >= 7:
        other = r + 1 - 2 * core
        cp = send(mis.at[1 - core], md, ds_sem, dr_sem, (other, c))
        cp.wait_recv()
        for i in range(X):
            send_x[i] = mis[core, i] + md[i]
    if stop >= 8:
        cps = []
        for k in range(1, X):
            t = lax.rem(x + k, X)
            cps.append(
                send(send_x.at[t], mx.at[k - 1], ms_sem.at[k], mr_sem.at[k], (t * 2 + core, c))
            )
        total = send_x[x]
        for k in range(1, X):
            cps[k - 1].wait_recv()
            total = total + mx[k - 1]
        for b in range(J):
            out_ref[b] = total[:, b * npar : (b + 1) * npar] + pbuf[r, b].astype(F32)
        for cp in gcps:
            cp.wait_recv()
        for q in range(R // 2):
            grad_ref[q : q + 1, :] = jnp.concatenate(
                [gbuf[2 * q, 0:1, :sens], gbuf[2 * q + 1, 0:1, :sens]], axis=1
            )
    elif stop >= 6:
        for cp in gcps:
            cp.wait_recv()
    if stop < 8:
        out_ref[...] = jnp.zeros_like(out_ref)
        grad_ref[...] = jnp.zeros_like(grad_ref)
    for cp in sends:
        cp.wait_send()


def per_device(R, Z, stop, probes, lag_blocks, sensor_weights, sensor_mask):
    npar = probes.shape[2]
    sens = NS // R
    rows, lanes = R * PROBES, J * sens
    X = R // 2
    dma = lambda n: pltpu.SemaphoreType.DMA((n,))
    out, grad = pl.pallas_call(
        functools.partial(kernel, R, Z, stop),
        out_shape=(
            jax.ShapeDtypeStruct((J, PROBES, npar), F32),
            jax.ShapeDtypeStruct((NS // 128, 128), F32),
        ),
        in_specs=[pl.BlockSpec(memory_space=pl.ANY)] * 2 + [pl.BlockSpec(memory_space=pltpu.VMEM)] * 2,
        out_specs=(pl.BlockSpec(memory_space=pltpu.VMEM),) * 2,
        scratch_shapes=[
            pltpu.VMEM((R, J, PROBES, npar), BF16),
            pltpu.VMEM((R, J, sens, npar), BF16),
            pltpu.VMEM((rows, lanes), F32),
            pltpu.VMEM((Y - 1, rows // Y, lanes), F32),
            pltpu.VMEM((Z, 16, 128), F32),
            pltpu.VMEM((Z - 1, 16, 128), F32),
            pltpu.VMEM((Z, 16, 128), BF16),
            pltpu.VMEM((Y, Z, 16, 128), BF16),
            pltpu.VMEM((2, X, PROBES, J * npar), F32),
            pltpu.VMEM((X, PROBES, J * npar), F32),
            pltpu.VMEM((X, PROBES, J * npar), F32),
            pltpu.VMEM((X - 1, PROBES, J * npar), F32),
            pltpu.VMEM((8, 128), F32),
            pltpu.VMEM((R, 8, 128), F32),
            dma(2), dma(R), dma(R), dma(R), dma(R), dma(Y), dma(Y), dma(Z), dma(Z),
            dma(Z), dma(Z), dma(Y), dma(Y),
            pltpu.SemaphoreType.DMA, pltpu.SemaphoreType.DMA, dma(X), dma(X), dma(R), dma(R),
        ],
        compiler_params=pltpu.CompilerParams(
            collective_id=0, has_side_effects=True, vmem_limit_bytes=48 * 1024 * 1024
        ),
        cost_estimate=pl.CostEstimate(flops=2 * 10**9, bytes_accessed=10**6, transcendentals=0),
        name="toeplitz",
    )(
        probes, lag_blocks,
        sensor_weights.reshape(NS // 128, 128), sensor_mask.reshape(NS // 128, 128),
    )
    return out, grad.reshape(NS)


def solution(mesh, stop=8):
    R, Z = mesh.shape["lag"], mesh.shape["par"] // Y
    return jax.shard_map(
        functools.partial(per_device, R, Z, stop),
        mesh=mesh,
        in_specs=(P("lag", None, "par"), P("lag", None, "par"), P(), P()),
        out_specs=(P("lag", None, "par"), P()),
        check_vma=False,
    )
```

time: 614 us -> 82.6 us (0.13)
  waiting for transfers between devices: 523 us -> 0 us
  Pallas kernels: 0 us -> 77.2 us
  other arithmetic: 25.5 us -> 0 us
  blocking collectives: 20.2 us -> 0 us
  local copies, waits for them, and re-layouts: 18 us -> 4.47 us
  between operations: 14.1 us -> 0.65 us
  matrix products: 11.7 us -> 0 us
    psum x1 -> x0, waiting for transfers between devices: 486 us -> none  [per_device(): observed = lax.psum(partial_obs, ('lag', 'par'))]
    pallas_call x0 -> x1, Pallas kernels: none -> 77.2 us  [per_device(): pl.pallas_call(functools.partial(kernel, R, Z, stop), out_shape=(jax.Shap...]
    reduce_scatter x1 -> x0, waiting for transfers between devices: 37.4 us -> none  [per_device(): lax.psum_scatter(product.reshape(lax.axis_size('lag') * LAG_DEV, PROBES,...]
    dynamic_update_slice x3 -> x0, other arithmetic: 20.4 us -> none  [per_device(): lax.dynamic_update_slice_in_dim(running, current + product[:, :, offset,...]
    all_gather x1 -> x0, blocking collectives: 20.2 us -> none  [per_device(): arrived = lax.all_gather(probes, 'lag', axis=0, tiled=True)]
    dot_general x2 -> x0, matrix products: 11.7 us -> none  [the longest x1 8.07 us: per_device(): lax.dot_general(arrived.reshape(num_rows * PROBES, width), stacked_blocks...]
  transfers between devices with their start and end apart: 2 -> 0, of which waited for: 2 -> 0; matrix products, arithmetic and copies ran while one was open for 0% -> 0% of each run, Pallas kernels for 0% -> 0%
where the time goes in v1:
time: 82.6 us; the launch traced here: 82.3 us
  Pallas kernels  77.2 us (93%)
  local copies, waits for them, and re-layouts  4.47 us (5%)
    pallas_call x1, Pallas kernels, per_device(): pl.pallas_call(functools.partial(kernel, R, Z, stop), out_shape=(jax.Shap...  77.2 us
    unnamed x10, local copies, waits for them, and re-layouts  4.47 us

profile of v1, /device:TPU:1, one launch (start us, length us, event | category | flops | bytes accessed | tf_op | source)
XLA Modules:
  0.0 82.3 jit_solution(318156444076527551)
XLA Ops:
  0.6 0.0 copy-start.2
  0.6 0.7 copy-done.2
  1.3 0.0 copy-start
  1.3 1.0 %copy-done = bf16[4,512,128]{2,1,0:T(8,128)(2,1)S(1)} copy-done((bf16[4,512,128]{2,1,0:T(8,128)(2,1)S(1)}, bf16[4,512,128]{2,1,0:T(8,128)(2,1)}, u32[]{:S(2)}) %copy-start) | copy-done | bytes 524312
  2.4 0.0 copy-start.1
  2.4 0.8 %copy-done.1 = bf16[4,64,128]{2,1,0:T(8,128)(2,1)S(1)} copy-done((bf16[4,64,128]{2,1,0:T(8,128)(2,1)S(1)}, bf16[4,64,128]{2,1,0:T(8,128)(2,1)}, u32[]{:S(2)}) %copy-start.1) | copy-done | bytes 65560
  3.2 0.0 copy-start.3
  3.2 0.7 copy-done.3
  3.9 77.2 %toeplitz.1 = (f32[4,64,128]{2,1,0:T(8,128)S(1)}, f32[4,128]{1,0:T(4,128)S(1)}) custom-call(bf16[4,64,128]{2,1,0:T(8,128)(2,1)S(1)} %copy-done.1, bf16[4,512,128]{2,1,0:T(8,128)(2,1)S(1)} %copy-done, f32[4,128]{1,0:T(4,128)S(1)} %bitcast.4, s32[4,128]{1,0:T(4,128)S(1)} %bitcast.5), custom_call_target="tpu_custom_call" | custom-call | flops 2000000000 | bytes 1000000 | tf_op jit(solution)/shard_map/toeplitz/pallas_call | solution.py:234
  81.1 0.7 copy.8
  81.8 0.6 copy.9
Async XLA Ops:
  0.6 0.7 copy-start.2
  1.3 1.0 %copy-start = (bf16[4,512,128]{2,1,0:T(8,128)(2,1)S(1)}, bf16[4,512,128]{2,1,0:T(8,128)(2,1)}, u32[]{:S(2)}) copy-start(bf16[4,512,128]{2,1,0:T(8,128)(2,1)} %lag_ref.1) | copy-start | bytes 1572868
  2.4 0.8 %copy-start.1 = (bf16[4,64,128]{2,1,0:T(8,128)(2,1)S(1)}, bf16[4,64,128]{2,1,0:T(8,128)(2,1)}, u32[]{:S(2)}) copy-start(bf16[4,64,128]{2,1,0:T(8,128)(2,1)} %probes_ref.1) | copy-start | bytes 196612
  3.2 0.7 copy-start.3

commit v2 on v0

v2 whole, which is shorter than its diff:
```python
import functools

import jax
import jax.numpy as jnp
from jax import lax
from jax.experimental import pallas as pl
from jax.experimental.pallas import tpu as pltpu
from jax.sharding import PartitionSpec as P

MESH = pl.DeviceIdType.MESH
NS = 512
PROBES = 64
J = 4
Y = 4
Z = 16
H = 2
Q = 4
F32 = jnp.float32
BF16 = jnp.bfloat16


def toeplitz_block(lags, d):
    rows = []
    for b in range(J):
        parts = []
        for c in range(J):
            l = J * d + b - c
            if l < 0:
                parts.append(jnp.zeros(lags.shape[-2:], BF16))
            else:
                parts.append(lags[l // J, l % J])
        rows.append(jnp.concatenate(parts, axis=1))
    return jnp.concatenate(rows, axis=0)


def kernel(
    R, stop,
    probes_ref, lag_ref, weight_hbm, mask_hbm,
    out_ref, grad_ref,
    pbuf, lbuf, weight_ref, mask_ref, obs, ry, sz, rz, wz, wy, mis, md, send_x, mx, gsend, gbuf,
    near_sem, local_sem, ps_sem, pr_sem, fs_sem, fr_sem, xs_sem, xr_sem, ys_sem, yr_sem,
    zs_sem, zr_sem, azs_sem, azr_sem, ays_sem, ayr_sem, ds_sem, dr_sem, ms_sem, mr_sem, gs_sem, gr_sem,
):
    r = lax.axis_index("lag")
    c = lax.axis_index("par")
    z, y = c // Y, lax.rem(c, Y)
    zq = z // Q
    x, core = r // 2, lax.rem(r, 2)
    X = R // 2
    sens = NS // R
    part = sens // H
    npar = pbuf.shape[-1]
    partner = (r + 1 - 2 * core, c)

    lag_peer = lambda k: (lax.rem(r + k, R), c)
    x_peer = lambda k: (lax.rem(x + k, X) * 2 + core, c)
    y_peer = lambda k: (r, z * Y + lax.rem(y + k, Y))
    z_at = lambda t: (r, t * Y + y)
    z_peer = lambda k: z_at(lax.rem(z + k + Z, Z))

    def signal(sem, dev):
        pl.semaphore_signal(sem, inc=1, device_id=dev, device_id_type=MESH)

    def remote(src, dst, ssem, rsem, dev):
        return pltpu.make_async_remote_copy(
            src_ref=src, dst_ref=dst, send_sem=ssem, recv_sem=rsem, device_id=dev, device_id_type=MESH
        )

    sends = []

    def send(*a):
        cp = remote(*a)
        cp.start()
        sends.append(cp)
        return cp

    local = [
        pltpu.make_async_copy(probes_ref, pbuf.at[r], local_sem.at[0]),
        pltpu.make_async_copy(weight_hbm, weight_ref, local_sem.at[1]),
        pltpu.make_async_copy(mask_hbm, mask_ref, local_sem.at[2]),
    ]

    def lag_part(q, h):
        return lag_ref.at[:, pl.ds(pl.multiple_of(q * sens + h * part, part), part), :]

    for h in range(H):
        local.append(pltpu.make_async_copy(lag_part(r, h), lbuf.at[h, r], local_sem.at[3 + h]))
    for cp in local:
        cp.start()

    barrier = pltpu.get_barrier_semaphore()
    for k in range(1, R):
        signal(barrier, lag_peer(k))
    for k in range(1, Y):
        signal(barrier, y_peer(k))
    for k in (1, -1):
        signal(barrier, z_peer(k))
    pl.semaphore_wait(barrier, R + Y)

    def near_signal(i):
        for k in (1 << i, -(1 << i)):
            signal(near_sem.at[i], z_peer(k))

    def near_wait(i):
        pl.semaphore_wait(near_sem.at[i], 2)

    near_signal(0)

    pcps = [send(probes_ref, pbuf.at[r], ps_sem.at[0], pr_sem.at[0], partner)]
    for k in (2, 1, 3):
        pcps.append(send(probes_ref, pbuf.at[r], ps_sem.at[k], pr_sem.at[k], x_peer(k)))
    lcps = [[], []]
    for h in range(H):
        for k in (4, 5, 3, 2, 6, 7, 1):
            q = lax.rem(r + k, R)
            lcps[h].append(send(lag_part(q, h), lbuf.at[h, r], xs_sem.at[h, k], xr_sem.at[h, k], (q, c)))
    near_wait(0)
    near_signal(1)
    fcps = []
    for k in (1, 3, 2):
        pcps[{2: 1, 1: 2, 3: 3}[k]].wait_recv()
        src = lax.rem(x - k + X, X) * 2 + core
        fcps.append(send(pbuf.at[src], pbuf.at[src], fs_sem.at[k], fr_sem.at[k], partner))
    near_wait(1)
    near_signal(2)
    for cp in local:
        cp.wait()
    pcps[0].wait_recv()
    for cp in fcps:
        cp.wait_recv()

    rows_y = R * PROBES // Y
    rows_q = rows_y // Q

    def forward(h):
        for cp in lcps[h]:
            cp.wait_recv()
        for d in range(R):
            n = R - d
            lhs = jnp.concatenate([pbuf[:n, b].reshape(n * PROBES, npar) for b in range(J)], axis=1)
            term = lax.dot_general(
                lhs, toeplitz_block(lbuf.at[h], d), (((1,), (1,)), ((), ())), preferred_element_type=F32
            )
            if d == 0:
                obs[h] = term
            else:
                obs[h, d * PROBES :, :] += term

    def quarter(o):
        return lax.rem(zq + o, Q)

    order = (2, 1, 3, 0)

    def sum_y_start(h):
        cps = []
        for i, o in enumerate(order):
            q = quarter(o)
            for k in range(1, Y):
                t = lax.rem(y + k, Y)
                cps.append(
                    send(
                        obs.at[h, pl.ds(pl.multiple_of(t * rows_y + q * rows_q, rows_q), rows_q), :],
                        ry.at[h, i, k - 1], ys_sem.at[h, i, k], yr_sem.at[h, i, k], y_peer(k),
                    )
                )
        return cps

    late = []

    def sum_z_start(h, ycps):
        for i, o in enumerate(order):
            q = quarter(o)
            total = obs[h, pl.ds(pl.multiple_of(y * rows_y + q * rows_q, rows_q), rows_q), :]
            for k in range(1, Y):
                ycps[i * (Y - 1) + k - 1].wait_recv()
                total = total + ry[h, i, k - 1]
            sz[h, i] = total
            for e in range(2):
                t = Q * q + 2 * e + h
                k = lax.rem(t - z + Z, Z)
                cp = remote(
                    sz.at[h, i, pl.ds(16 * e, 16), :], rz.at[k],
                    zs_sem.at[h, i, e], zr_sem.at[k], z_at(t),
                )
                if o:
                    cp.start()
                    sends.append(cp)
                else:
                    pl.when(t != z)(cp.start)
                    late.append((t != z, cp))

    forward(0)
    ycps0 = sum_y_start(0)
    forward(1)
    ycps1 = sum_y_start(1)
    near_wait(2)
    sum_z_start(0, ycps0)
    sum_z_start(1, ycps1)

    hz = lax.rem(z, H)
    row = weight_ref[pl.ds(r // 2, 1), :]
    on = mask_ref[pl.ds(r // 2, 1), :].astype(F32)
    own = sz[hz, 3, pl.ds(pl.multiple_of(16 * (lax.rem(z, Q) // 2), 16), 16), :]
    for k in range(1, Z):
        remote(rz.at[k], rz.at[k], zs_sem.at[0, 0, 0], zr_sem.at[k], z_peer(k)).wait_recv()
        own = own + rz[k]
    both = row * on
    scale = jnp.zeros((1, 128), F32)
    for j in range(4):
        piece = both[:, j * part : (j + 1) * part]
        piece = jnp.concatenate([piece] * J, axis=1)
        scale = jnp.where(core * H + hz == j, piece, scale)
    wz[z] = (scale * own).astype(BF16)
    for k in (8, 7, 9, 6, 10, 5, 11, 4, 12, 3, 13, 2, 14, 1, 15):
        send(wz.at[z], wz.at[z], azs_sem.at[k], azr_sem.at[z], z_peer(k))
    aycps = []
    for i, o in enumerate((0, 1, 3, 2)):
        q = quarter(o)
        for e in range(Q):
            t = Q * q + e
            cp = remote(wz.at[t], wz.at[t], azs_sem.at[1], azr_sem.at[t], z_at(t))
            if o:
                cp.wait_recv()
            else:
                pl.when(t != z)(cp.wait_recv)
        rng = pl.ds(Q * q, Q)
        for k in range(1, Y):
            aycps.append(send(wz.at[rng], wy.at[y, rng], ays_sem.at[i, k], ayr_sem.at[i, k], y_peer(k)))
    wy[y] = wz[...]
    for cp in aycps:
        cp.wait_recv()

    def wrow(a):
        i, g = a * PROBES // rows_y, (a * PROBES % rows_y) // 16
        return jnp.concatenate(
            [jnp.concatenate([wy[i, 2 * (g + q)], wy[i, 2 * (g + q) + 1]], axis=1) for q in range(PROBES // 16)],
            axis=0,
        )

    wfull = [wrow(a) for a in range(R)]
    for d in range(R):
        n = R - d
        rhs = jnp.concatenate([toeplitz_block(lbuf.at[h], d) for h in range(H)], axis=0)
        term = jnp.dot(jnp.concatenate(wfull[d:], axis=0), rhs, preferred_element_type=F32)
        for a in range(n):
            piece = term[a * PROBES : (a + 1) * PROBES]
            if d == 0:
                mis[a % 2, a // 2] = piece
            else:
                mis[a % 2, a // 2] += piece

    dcps = []
    for k in (2, 1, 3, 0):
        t = lax.rem(x + k, X)
        dcps.append(send(mis.at[1 - core, t], md.at[k], ds_sem.at[k], dr_sem.at[k], partner))

    def mine(v):
        return jnp.where(core == 0, v[:, :sens], v[:, sens:])

    tot = [jnp.zeros((16, 128), F32) for _ in range(H)]
    for i in range(Y):
        for j in range(Z):
            w = wy[i, j].astype(F32)
            tot[j % H] = tot[j % H] + w * w
    sq = []
    for h in range(H):
        v = jnp.sum(tot[h], axis=0, keepdims=True)
        sq.append(sum(v[:, b * part : (b + 1) * part] for b in range(J)))
    sq = jnp.concatenate(sq, axis=1)
    wr = mine(row)
    g = mine(on) * sq / (wr * wr) * (1.0 / (R * J * PROBES))
    gsend[...] = jnp.broadcast_to(jnp.concatenate([g, g], axis=1), (8, 128))
    gcps = []
    for k in range(1, R):
        gcps.append(send(gsend, gbuf.at[r], gs_sem.at[k], gr_sem.at[k], lag_peer(k)))
    gbuf[r] = gsend[...]

    mcps = []
    for i, k in enumerate((2, 1, 3)):
        t = lax.rem(x + k, X)
        dcps[i].wait_recv()
        send_x[k] = (mis[core, t] + md[k]).astype(BF16)
        mcps.append(send(send_x.at[k], mx.at[k], ms_sem.at[k], mr_sem.at[k], x_peer(k)))
    dcps[3].wait_recv()
    total = mis[core, x] + md[0]
    total = total + jnp.concatenate([pbuf[r, b].astype(F32) for b in range(J)], axis=1)
    for i, k in ((1, 1), (2, 3), (0, 2)):
        mcps[i].wait_recv()
        total = total + mx[k].astype(F32)
    for b in range(J):
        out_ref[b] = total[:, b * npar : (b + 1) * npar]
    for cp in gcps:
        cp.wait_recv()
    for q in range(R // 2):
        grad_ref[q : q + 1, :] = jnp.concatenate([gbuf[2 * q, 0:1, :sens], gbuf[2 * q + 1, 0:1, :sens]], axis=1)
    for cp in sends:
        cp.wait_send()
    for cond, cp in late:
        pl.when(cond)(cp.wait_send)


def per_device(R, stop, probes, lag_blocks, sensor_weights, sensor_mask):
    npar = probes.shape[2]
    sens = NS // R
    part = sens // H
    rows = R * PROBES
    X = R // 2
    dma = lambda *n: pltpu.SemaphoreType.DMA(n)
    out, grad = pl.pallas_call(
        functools.partial(kernel, R, stop),
        out_shape=(
            jax.ShapeDtypeStruct((J, PROBES, npar), F32),
            jax.ShapeDtypeStruct((NS // 128, 128), F32),
        ),
        in_specs=[pl.BlockSpec(memory_space=pltpu.HBM)] * 4,
        out_specs=(pl.BlockSpec(memory_space=pltpu.VMEM),) * 2,
        scratch_shapes=[
            pltpu.VMEM((R, J, PROBES, npar), BF16),
            pltpu.VMEM((H, R, J, part, npar), BF16),
            pltpu.VMEM((NS // 128, 128), F32),
            pltpu.VMEM((NS // 128, 128), jnp.int32),
            pltpu.VMEM((H, rows, 128), F32),
            pltpu.VMEM((H, Q, Y - 1, rows // Y // Q, 128), F32),
            pltpu.VMEM((H, Q, rows // Y // Q, 128), F32),
            pltpu.VMEM((Z, 16, 128), F32),
            pltpu.VMEM((Z, 16, 128), BF16),
            pltpu.VMEM((Y, Z, 16, 128), BF16),
            pltpu.VMEM((2, X, PROBES, J * npar), F32),
            pltpu.VMEM((X, PROBES, J * npar), F32),
            pltpu.VMEM((X, PROBES, J * npar), BF16),
            pltpu.VMEM((X, PROBES, J * npar), BF16),
            pltpu.VMEM((8, 128), F32),
            pltpu.VMEM((R, 8, 128), F32),
            pltpu.SemaphoreType.REGULAR((3,)),
            dma(5), dma(X), dma(X), dma(X), dma(X), dma(H, R), dma(H, R), dma(H, Q, Y), dma(H, Q, Y),
            dma(H, Q, 2), dma(Z), dma(Z), dma(Z), dma(Q, Y), dma(Q, Y), dma(X), dma(X), dma(X), dma(X),
            dma(R), dma(R),
        ],
        compiler_params=pltpu.CompilerParams(
            collective_id=0, has_side_effects=True, vmem_limit_bytes=48 * 1024 * 1024
        ),
        cost_estimate=pl.CostEstimate(flops=2 * 10**9, bytes_accessed=10**6, transcendentals=0),
        name="toeplitz",
    )(
        probes, lag_blocks,
        sensor_weights.reshape(NS // 128, 128), sensor_mask.reshape(NS // 128, 128),
    )
    return out, grad.reshape(NS)


def solution(mesh, stop=8):
    R = mesh.shape["lag"]
    return jax.shard_map(
        functools.partial(per_device, R, stop),
        mesh=mesh,
        in_specs=(P("lag", None, "par"), P("lag", None, "par"), P(), P()),
        out_specs=(P("lag", None, "par"), P()),
        check_vma=False,
    )
```

time: 614 us -> 63.8 us (0.10)
  waiting for transfers between devices: 523 us -> 0 us
  Pallas kernels: 0 us -> 58.4 us
  other arithmetic: 25.5 us -> 0 us
  blocking collectives: 20.2 us -> 0 us
  local copies, waits for them, and re-layouts: 18 us -> 4.47 us
  between operations: 14.1 us -> 0.65 us
  matrix products: 11.7 us -> 0 us
    psum x1 -> x0, waiting for transfers between devices: 486 us -> none  [per_device(): observed = lax.psum(partial_obs, ('lag', 'par'))]
    pallas_call x0 -> x1, Pallas kernels: none -> 58.4 us  [per_device(): pl.pallas_call(functools.partial(kernel, R, stop), out_shape=(jax.ShapeDt...]
    reduce_scatter x1 -> x0, waiting for transfers between devices: 37.4 us -> none  [per_device(): lax.psum_scatter(product.reshape(lax.axis_size('lag') * LAG_DEV, PROBES,...]
    dynamic_update_slice x3 -> x0, other arithmetic: 20.4 us -> none  [per_device(): lax.dynamic_update_slice_in_dim(running, current + product[:, :, offset,...]
    all_gather x1 -> x0, blocking collectives: 20.2 us -> none  [per_device(): arrived = lax.all_gather(probes, 'lag', axis=0, tiled=True)]
    dot_general x2 -> x0, matrix products: 11.7 us -> none  [the longest x1 8.07 us: per_device(): lax.dot_general(arrived.reshape(num_rows * PROBES, width), stacked_blocks...]
  transfers between devices with their start and end apart: 2 -> 0, of which waited for: 2 -> 0; matrix products, arithmetic and copies ran while one was open for 0% -> 0% of each run, Pallas kernels for 0% -> 0%
where the time goes in v2:
time: 63.8 us; the launch traced here: 63.5 us
  Pallas kernels  58.4 us (92%)
  local copies, waits for them, and re-layouts  4.47 us (7%)
  between operations  0.65 us (1%)
    pallas_call x1, Pallas kernels, per_device(): pl.pallas_call(functools.partial(kernel, R, stop), out_shape=(jax.ShapeDt...  58.4 us
    unnamed x10, local copies, waits for them, and re-layouts  4.47 us

profile of v2, /device:TPU:1, one launch (start us, length us, event | category | flops | bytes accessed | tf_op | source)
XLA Modules:
  0.0 63.5 jit_solution(13055487651274097954)
XLA Ops:
  0.6 0.0 copy-start.2
  0.6 0.7 %copy-done.2 = f32[512]{0:T(512)S(1)} copy-done((f32[512]{0:T(512)S(1)}, f32[512]{0:T(512)}, u32[]{:S(2)}) %copy-start.2) | copy-done | bytes 2072
  1.3 0.0 copy-start
  1.3 1.0 %copy-done = bf16[4,512,128]{2,1,0:T(8,128)(2,1)S(1)} copy-done((bf16[4,512,128]{2,1,0:T(8,128)(2,1)S(1)}, bf16[4,512,128]{2,1,0:T(8,128)(2,1)}, u32[]{:S(2)}) %copy-start) | copy-done | bytes 524312
  2.4 0.0 copy-start.1
  2.4 0.8 %copy-done.1 = bf16[4,64,128]{2,1,0:T(8,128)(2,1)S(1)} copy-done((bf16[4,64,128]{2,1,0:T(8,128)(2,1)S(1)}, bf16[4,64,128]{2,1,0:T(8,128)(2,1)}, u32[]{:S(2)}) %copy-start.1) | copy-done | bytes 65560
  3.2 0.0 copy-start.3
  3.2 0.7 %copy-done.3 = s32[512]{0:T(512)S(1)} copy-done((s32[512]{0:T(512)S(1)}, s32[512]{0:T(512)}, u32[]{:S(2)}) %copy-start.3) | copy-done | bytes 2072
  3.9 58.4 %toeplitz.1 = (f32[4,64,128]{2,1,0:T(8,128)S(1)}, f32[4,128]{1,0:T(4,128)S(1)}) custom-call(bf16[4,64,128]{2,1,0:T(8,128)(2,1)S(1)} %copy-done.1, bf16[4,512,128]{2,1,0:T(8,128)(2,1)S(1)} %copy-done, f32[4,128]{1,0:T(4,128)S(1)} %bitcast.4, s32[4,128]{1,0:T(4,128)S(1)} %bitcast.5), custom_call_target="tpu_custom_call" | custom-call | flops 2000000000 | bytes 1000000 | tf_op jit(solution)/shard_map/toeplitz/pallas_call | solution.py:309
  62.3 0.7 %copy.8 = f32[4,64,128]{2,1,0:T(8,128)} copy(f32[4,64,128]{2,1,0:T(8,128)S(1)} %get-tuple-element.8) | data formatting | bytes 262144
  63.0 0.6 copy.9
Async XLA Ops:
  0.6 0.7 %copy-start.2 = (f32[512]{0:T(512)S(1)}, f32[512]{0:T(512)}, u32[]{:S(2)}) copy-start(f32[512]{0:T(512)} %param.6) | copy-start | bytes 6148
  1.3 1.0 %copy-start = (bf16[4,512,128]{2,1,0:T(8,128)(2,1)S(1)}, bf16[4,512,128]{2,1,0:T(8,128)(2,1)}, u32[]{:S(2)}) copy-start(bf16[4,512,128]{2,1,0:T(8,128)(2,1)} %lag_ref.1) | copy-start | bytes 1572868
  2.4 0.8 %copy-start.1 = (bf16[4,64,128]{2,1,0:T(8,128)(2,1)S(1)}, bf16[4,64,128]{2,1,0:T(8,128)(2,1)}, u32[]{:S(2)}) copy-start(bf16[4,64,128]{2,1,0:T(8,128)(2,1)} %probes_ref.1) | copy-start | bytes 196612
  3.2 0.7 %copy-start.3 = (s32[512]{0:T(512)S(1)}, s32[512]{0:T(512)}, u32[]{:S(2)}) copy-start(s32[512]{0:T(512)} %param.7) | copy-start | bytes 6148

commit v3 on v2

--- a/solution.py
+++ b/solution.py
@@ -129,78 +129,86 @@
     for cp in fcps:
         cp.wait_recv()
 
-    rows_y = R * PROBES // Y
-    rows_q = rows_y // Q
-
-    def forward(h):
-        for cp in lcps[h]:
-            cp.wait_recv()
+    rows = PROBES // Q
+
+    def forward(h, start, count):
+        acc = None
         for d in range(R):
             n = R - d
-            lhs = jnp.concatenate([pbuf[:n, b].reshape(n * PROBES, npar) for b in range(J)], axis=1)
+            lhs = jnp.concatenate(
+                [pbuf[:n, b, pl.ds(start, count), :].reshape(n * count, npar) for b in range(J)], axis=1
+            )
             term = lax.dot_general(
                 lhs, toeplitz_block(lbuf.at[h], d), (((1,), (1,)), ((), ())), preferred_element_type=F32
-            )
+            ).reshape(n, count, 128)
             if d == 0:
-                obs[h] = term
+                acc = [term[a] for a in range(R)]
             else:
-                obs[h, d * PROBES :, :] += term
+                for a in range(n):
+                    acc[a + d] = acc[a + d] + term[a]
+        for a in range(R):
+            obs[h, a, pl.ds(start, count), :] = acc[a]
 
     def quarter(o):
         return lax.rem(zq + o, Q)
 
+    def probes_of(q):
+        return pl.ds(pl.multiple_of(q * rows, rows), rows)
+
     order = (2, 1, 3, 0)
 
-    def sum_y_start(h):
+    def sum_y_start(h, i):
+        q = quarter(order[i])
         cps = []
-        for i, o in enumerate(order):
-            q = quarter(o)
-            for k in range(1, Y):
-                t = lax.rem(y + k, Y)
-                cps.append(
-                    send(
-                        obs.at[h, pl.ds(pl.multiple_of(t * rows_y + q * rows_q, rows_q), rows_q), :],
-                        ry.at[h, i, k - 1], ys_sem.at[h, i, k], yr_sem.at[h, i, k], y_peer(k),
-                    )
+        for k in range(1, Y):
+            t = lax.rem(y + k, Y)
+            cps.append(
+                send(
+                    obs.at[h, pl.ds(2 * t, 2), probes_of(q), :],
+                    ry.at[h, i, k - 1], ys_sem.at[h, i, k], yr_sem.at[h, i, k], y_peer(k),
                 )
+            )
         return cps
 
     late = []
 
-    def sum_z_start(h, ycps):
-        for i, o in enumerate(order):
-            q = quarter(o)
-            total = obs[h, pl.ds(pl.multiple_of(y * rows_y + q * rows_q, rows_q), rows_q), :]
-            for k in range(1, Y):
-                ycps[i * (Y - 1) + k - 1].wait_recv()
-                total = total + ry[h, i, k - 1]
-            sz[h, i] = total
-            for e in range(2):
-                t = Q * q + 2 * e + h
-                k = lax.rem(t - z + Z, Z)
-                cp = remote(
-                    sz.at[h, i, pl.ds(16 * e, 16), :], rz.at[k],
-                    zs_sem.at[h, i, e], zr_sem.at[k], z_at(t),
-                )
-                if o:
-                    cp.start()
-                    sends.append(cp)
-                else:
-                    pl.when(t != z)(cp.start)
-                    late.append((t != z, cp))
-
-    forward(0)
-    ycps0 = sum_y_start(0)
-    forward(1)
-    ycps1 = sum_y_start(1)
+    def sum_z_start(h, i, ycps):
+        o = order[i]
+        q = quarter(o)
+        total = obs[h, pl.ds(2 * y, 2), probes_of(q), :]
+        for k in range(1, Y):
+            ycps[k - 1].wait_recv()
+            total = total + ry[h, i, k - 1]
+        sz[h, i] = total
+        for e in range(2):
+            t = Q * q + 2 * e + h
+            k = lax.rem(t - z + Z, Z)
+            cp = remote(sz.at[h, i, e], rz.at[k], zs_sem.at[h, i, e], zr_sem.at[k], z_at(t))
+            if o:
+                cp.start()
+                sends.append(cp)
+            else:
+                pl.when(t != z)(cp.start)
+                late.append((t != z, cp))
+
+    for cp in lcps[0]:
+        cp.wait_recv()
+    forward(0, 0, PROBES)
+    ycps = [[sum_y_start(0, i) for i in range(Q)], []]
+    for cp in lcps[1]:
+        cp.wait_recv()
+    for i in range(Q):
+        forward(1, quarter(order[i]) * rows, rows)
+        ycps[1].append(sum_y_start(1, i))
     near_wait(2)
-    sum_z_start(0, ycps0)
-    sum_z_start(1, ycps1)
+    for h in range(H):
+        for i in range(Q):
+            sum_z_start(h, i, ycps[h][i])
 
     hz = lax.rem(z, H)
     row = weight_ref[pl.ds(r // 2, 1), :]
     on = mask_ref[pl.ds(r // 2, 1), :].astype(F32)
-    own = sz[hz, 3, pl.ds(pl.multiple_of(16 * (lax.rem(z, Q) // 2), 16), 16), :]
+    own = sz[hz, 3, lax.rem(z, Q) // 2]
     for k in range(1, Z):
         remote(rz.at[k], rz.at[k], zs_sem.at[0, 0, 0], zr_sem.at[k], z_peer(k)).wait_recv()
         own = own + rz[k]
@@ -213,8 +221,9 @@
     wz[z] = (scale * own).astype(BF16)
     for k in (8, 7, 9, 6, 10, 5, 11, 4, 12, 3, 13, 2, 14, 1, 15):
         send(wz.at[z], wz.at[z], azs_sem.at[k], azr_sem.at[z], z_peer(k))
+    arrive = (0, 1, 3, 2)
     aycps = []
-    for i, o in enumerate((0, 1, 3, 2)):
+    for i, o in enumerate(arrive):
         q = quarter(o)
         for e in range(Q):
             t = Q * q + e
@@ -223,45 +232,66 @@
                 cp.wait_recv()
             else:
                 pl.when(t != z)(cp.wait_recv)
-        rng = pl.ds(Q * q, Q)
+        aycps.append([])
         for k in range(1, Y):
-            aycps.append(send(wz.at[rng], wy.at[y, rng], ays_sem.at[i, k], ayr_sem.at[i, k], y_peer(k)))
-    wy[y] = wz[...]
-    for cp in aycps:
-        cp.wait_recv()
-
-    def wrow(a):
-        i, g = a * PROBES // rows_y, (a * PROBES % rows_y) // 16
-        return jnp.concatenate(
-            [jnp.concatenate([wy[i, 2 * (g + q)], wy[i, 2 * (g + q) + 1]], axis=1) for q in range(PROBES // 16)],
-            axis=0,
-        )
-
-    wfull = [wrow(a) for a in range(R)]
-    for d in range(R):
-        n = R - d
-        rhs = jnp.concatenate([toeplitz_block(lbuf.at[h], d) for h in range(H)], axis=0)
-        term = jnp.dot(jnp.concatenate(wfull[d:], axis=0), rhs, preferred_element_type=F32)
-        for a in range(n):
-            piece = term[a * PROBES : (a + 1) * PROBES]
-            if d == 0:
-                mis[a % 2, a // 2] = piece
-            else:
-                mis[a % 2, a // 2] += piece
-
-    dcps = []
-    for k in (2, 1, 3, 0):
-        t = lax.rem(x + k, X)
-        dcps.append(send(mis.at[1 - core, t], md.at[k], ds_sem.at[k], dr_sem.at[k], partner))
+            aycps[i].append(
+                send(wz.at[pl.ds(Q * q, Q)], wy.at[q, y], ays_sem.at[i, k], ayr_sem.at[i, k], y_peer(k))
+            )
+        wy[q, y] = wz[pl.ds(Q * q, Q)]
+
+    tot = [jnp.zeros((rows, 128), F32) for _ in range(H)]
+    half = J * npar // 2
+
+    def adjoint(i):
+        q = quarter(arrive[i])
+        for cp in aycps[i]:
+            cp.wait_recv()
+        w = []
+        for a in range(R):
+            e = 2 * (a % 2)
+            w.append(jnp.concatenate([wy[q, a // 2, e], wy[q, a // 2, e + 1]], axis=1))
+        for u in range(2):
+            acc = None
+            for d in range(R):
+                n = R - d
+                rhs = jnp.concatenate(
+                    [toeplitz_block(lbuf.at[h], d)[:, u * half : (u + 1) * half] for h in range(H)], axis=0
+                )
+                term = jnp.dot(jnp.concatenate(w[d:], axis=0), rhs, preferred_element_type=F32)
+                pieces = [term[a * rows : (a + 1) * rows] for a in range(n)]
+                acc = pieces if d == 0 else [acc[a] + pieces[a] for a in range(n)] + acc[n:]
+            for a in range(R):
+                mis[i, a % 2, a // 2, :, u * half : (u + 1) * half] = acc[a]
+        cps = []
+        for k in (2, 1, 3, 0):
+            t = lax.rem(x + k, X)
+            cps.append(
+                send(mis.at[i, 1 - core, t], md.at[i, k], ds_sem.at[i, k], dr_sem.at[i, k], partner)
+            )
+        for a in range(R):
+            for h in range(H):
+                v = w[a][:, 128 * h : 128 * h + 128].astype(F32)
+                tot[h] = tot[h] + v * v
+        return cps
+
+    def sum_x_start(i, dcps):
+        cps = []
+        for n, k in enumerate((2, 1, 3)):
+            t = lax.rem(x + k, X)
+            dcps[n].wait_recv()
+            send_x[i, k] = (mis[i, core, t] + md[i, k]).astype(BF16)
+            cps.append(send(send_x.at[i, k], mx.at[i, k], ms_sem.at[i, k], mr_sem.at[i, k], x_peer(k)))
+        return cps
+
+    dcps, mcps = [], []
+    for i in range(Q):
+        dcps.append(adjoint(i))
+        if i:
+            mcps.append(sum_x_start(i - 1, dcps[i - 1]))
 
     def mine(v):
         return jnp.where(core == 0, v[:, :sens], v[:, sens:])
 
-    tot = [jnp.zeros((16, 128), F32) for _ in range(H)]
-    for i in range(Y):
-        for j in range(Z):
-            w = wy[i, j].astype(F32)
-            tot[j % H] = tot[j % H] + w * w
     sq = []
     for h in range(H):
         v = jnp.sum(tot[h], axis=0, keepdims=True)
@@ -275,20 +305,17 @@
         gcps.append(send(gsend, gbuf.at[r], gs_sem.at[k], gr_sem.at[k], lag_peer(k)))
     gbuf[r] = gsend[...]
 
-    mcps = []
-    for i, k in enumerate((2, 1, 3)):
-        t = lax.rem(x + k, X)
-        dcps[i].wait_recv()
-        send_x[k] = (mis[core, t] + md[k]).astype(BF16)
-        mcps.append(send(send_x.at[k], mx.at[k], ms_sem.at[k], mr_sem.at[k], x_peer(k)))
-    dcps[3].wait_recv()
-    total = mis[core, x] + md[0]
-    total = total + jnp.concatenate([pbuf[r, b].astype(F32) for b in range(J)], axis=1)
-    for i, k in ((1, 1), (2, 3), (0, 2)):
-        mcps[i].wait_recv()
-        total = total + mx[k].astype(F32)
-    for b in range(J):
-        out_ref[b] = total[:, b * npar : (b + 1) * npar]
+    mcps.append(sum_x_start(Q - 1, dcps[Q - 1]))
+    for i in range(Q):
+        at = probes_of(quarter(arrive[i]))
+        dcps[i][3].wait_recv()
+        total = mis[i, core, x] + md[i, 0]
+        total = total + jnp.concatenate([pbuf[r, b, at, :].astype(F32) for b in range(J)], axis=1)
+        for n, k in ((1, 1), (2, 3), (0, 2)):
+            mcps[i][n].wait_recv()
+            total = total + mx[i, k].astype(F32)
+        for b in range(J):
+            out_ref[b, at, :] = total[:, b * npar : (b + 1) * npar]
     for cp in gcps:
         cp.wait_recv()
     for q in range(R // 2):
@@ -303,7 +330,6 @@
     npar = probes.shape[2]
     sens = NS // R
     part = sens // H
-    rows = R * PROBES
     X = R // 2
     dma = lambda *n: pltpu.SemaphoreType.DMA(n)
     out, grad = pl.pallas_call(
@@ -319,21 +345,21 @@
             pltpu.VMEM((H, R, J, part, npar), BF16),
             pltpu.VMEM((NS // 128, 128), F32),
             pltpu.VMEM((NS // 128, 128), jnp.int32),
-            pltpu.VMEM((H, rows, 128), F32),
-            pltpu.VMEM((H, Q, Y - 1, rows // Y // Q, 128), F32),
-            pltpu.VMEM((H, Q, rows // Y // Q, 128), F32),
+            pltpu.VMEM((H, R, PROBES, 128), F32),
+            pltpu.VMEM((H, Q, Y - 1, 2, PROBES // Q, 128), F32),
+            pltpu.VMEM((H, Q, 2, PROBES // Q, 128), F32),
             pltpu.VMEM((Z, 16, 128), F32),
             pltpu.VMEM((Z, 16, 128), BF16),
-            pltpu.VMEM((Y, Z, 16, 128), BF16),
-            pltpu.VMEM((2, X, PROBES, J * npar), F32),
-            pltpu.VMEM((X, PROBES, J * npar), F32),
-            pltpu.VMEM((X, PROBES, J * npar), BF16),
-            pltpu.VMEM((X, PROBES, J * npar), BF16),
+            pltpu.VMEM((Q, Y, Q, 16, 128), BF16),
+            pltpu.VMEM((Q, 2, X, PROBES // Q, J * npar), F32),
+            pltpu.VMEM((Q, X, PROBES // Q, J * npar), F32),
+            pltpu.VMEM((Q, X, PROBES // Q, J * npar), BF16),
+            pltpu.VMEM((Q, X, PROBES // Q, J * npar), BF16),
             pltpu.VMEM((8, 128), F32),
             pltpu.VMEM((R, 8, 128), F32),
             pltpu.SemaphoreType.REGULAR((3,)),
             dma(5), dma(X), dma(X), dma(X), dma(X), dma(H, R), dma(H, R), dma(H, Q, Y), dma(H, Q, Y),
-            dma(H, Q, 2), dma(Z), dma(Z), dma(Z), dma(Q, Y), dma(Q, Y), dma(X), dma(X), dma(X), dma(X),
+            dma(H, Q, 2), dma(Z), dma(Z), dma(Z), dma(Q, Y), dma(Q, Y), dma(Q, X), dma(Q, X), dma(Q, X), dma(Q, X),
             dma(R), dma(R),
         ],
         compiler_params=pltpu.CompilerParams(
@@ -342,8 +368,10 @@
         cost_estimate=pl.CostEstimate(flops=2 * 10**9, bytes_accessed=10**6, transcendentals=0),
         name="toeplitz",
     )(
-        probes, lag_blocks,
-        sensor_weights.reshape(NS // 128, 128), sensor_mask.reshape(NS // 128, 128),
+        *(
+            pltpu.with_memory_space_constraint(v, pltpu.HBM)
+            for v in (probes, lag_blocks, sensor_weights.reshape(NS // 128, 128), sensor_mask.reshape(NS // 128, 128))
+        )
     )
     return out, grad.reshape(NS)
 

time: 63.8 us -> 59.7 us (0.936)
  local copies, waits for them, and re-layouts: 4.47 us -> 1.24 us
  Pallas kernels: 58.4 us -> 57.7 us
    unnamed x10 -> x2, local copies, waits for them, and re-layouts: 4.47 us -> 1.24 us
    pallas_call x1, Pallas kernels: 58.4 us -> 57.7 us  [per_device(): pl.pallas_call(functools.partial(kernel, R, stop), out_shape=(jax.ShapeDt...]
where the time goes in v3:
time: 59.7 us; the launch traced here: 59.6 us
  Pallas kernels  57.7 us (97%)
  local copies, waits for them, and re-layouts  1.24 us (2%)
  between operations  0.64 us (1%)
    pallas_call x1, Pallas kernels, per_device(): pl.pallas_call(functools.partial(kernel, R, stop), out_shape=(jax.ShapeDt...  57.7 us
    unnamed x2, local copies, waits for them, and re-layouts  1.24 us

profile of v3, /device:TPU:1, one launch (start us, length us, event | category | flops | bytes accessed | tf_op | source)
XLA Modules:
  0.0 59.6 jit_solution(6658598678094287509)
XLA Ops:
  0.6 57.7 %toeplitz.1 = (f32[4,64,128]{2,1,0:T(8,128)S(1)}, f32[4,128]{1,0:T(4,128)S(1)}) custom-call(bf16[4,64,128]{2,1,0:T(8,128)(2,1)} %probes_ref.1, bf16[4,512,128]{2,1,0:T(8,128)(2,1)} %lag_ref.1, f32[4,128]{1,0:T(4,128)} %bitcast.4, s32[4,128]{1,0:T(4,128)} %bitcast.5), custom_call_target="tpu_custom_call" | custom-call | flops 2000000000 | bytes 1000000 | tf_op jit(solution)/shard_map/toeplitz/pallas_call | solution.py:335
  58.4 0.7 %copy.8 = f32[4,64,128]{2,1,0:T(8,128)} copy(f32[4,64,128]{2,1,0:T(8,128)S(1)} %get-tuple-element.8) | data formatting | bytes 262144
  59.0 0.6 copy.9

commit v4 on v3

--- a/solution.py
+++ b/solution.py
@@ -206,8 +206,15 @@
             sum_z_start(h, i, ycps[h][i])
 
     hz = lax.rem(z, H)
-    row = weight_ref[pl.ds(r // 2, 1), :]
-    on = mask_ref[pl.ds(r // 2, 1), :].astype(F32)
+
+    def chip_row(v):
+        out = v[0:1, :]
+        for i in range(1, X):
+            out = jnp.where(x == i, v[i : i + 1, :], out)
+        return out
+
+    row = chip_row(weight_ref[...])
+    on = chip_row(mask_ref[...].astype(F32))
     own = sz[hz, 3, lax.rem(z, Q) // 2]
     for k in range(1, Z):
         remote(rz.at[k], rz.at[k], zs_sem.at[0, 0, 0], zr_sem.at[k], z_peer(k)).wait_recv()
@@ -318,8 +325,9 @@
             out_ref[b, at, :] = total[:, b * npar : (b + 1) * npar]
     for cp in gcps:
         cp.wait_recv()
-    for q in range(R // 2):
-        grad_ref[q : q + 1, :] = jnp.concatenate([gbuf[2 * q, 0:1, :sens], gbuf[2 * q + 1, 0:1, :sens]], axis=1)
+    grad_ref[...] = jnp.concatenate(
+        [jnp.concatenate([gbuf[2 * q, 0:1, :sens], gbuf[2 * q + 1, 0:1, :sens]], axis=1) for q in range(X)], axis=0
+    )
     for cp in sends:
         cp.wait_send()
     for cond, cp in late:

time: 59.7 us -> 59.7 us (level)
  no operation moved by 1% of the time
where the time goes in v4:
time: 59.7 us; the launch traced here: 59.6 us
  Pallas kernels  57.7 us (97%)
  local copies, waits for them, and re-layouts  1.24 us (2%)
  between operations  0.64 us (1%)
    pallas_call x1, Pallas kernels, per_device(): pl.pallas_call(functools.partial(kernel, R, stop), out_shape=(jax.ShapeDt...  57.7 us
    unnamed x2, local copies, waits for them, and re-layouts  1.24 us

profile of v4, /device:TPU:1, one launch (start us, length us, event | category | flops | bytes accessed | tf_op | source)
XLA Modules:
  0.0 59.6 jit_solution(312496066990838656)
XLA Ops:
  0.6 57.7 %toeplitz.1 = (f32[4,64,128]{2,1,0:T(8,128)S(1)}, f32[4,128]{1,0:T(4,128)S(1)}) custom-call(bf16[4,64,128]{2,1,0:T(8,128)(2,1)} %probes_ref.1, bf16[4,512,128]{2,1,0:T(8,128)(2,1)} %lag_ref.1, f32[4,128]{1,0:T(4,128)} %bitcast.4, s32[4,128]{1,0:T(4,128)} %bitcast.5), custom_call_target="tpu_custom_call" | custom-call | flops 2000000000 | bytes 1000000 | tf_op jit(solution)/shard_map/toeplitz/pallas_call | solution.py:343
  58.4 0.7 %copy.8 = f32[4,64,128]{2,1,0:T(8,128)} copy(f32[4,64,128]{2,1,0:T(8,128)S(1)} %get-tuple-element.8) | data formatting | bytes 262144
  59.0 0.6 copy.9
